TPU v7x, 32 devices: a whole 2x2x4 slice. The times are simulated.
32 devices in a mesh: groups: 2 (over y), seq: 8 (over z, x), head: 2 (over core).
Axes of the slice: x: 2, y: 2, z: 4, core: 2. Of those that a mesh axis runs over, the one named last changes fastest.
Arguments:
- queries: bfloat16 [2048, 4096], P(('groups', 'seq'), 'head'), parts along dimension 0, may hold values from -6 to 6
- key_rows: bfloat16 [2048, 4096], P(('groups', 'seq'), 'head'), parts along dimension 0, may hold values from -6 to 6
- value_rows: bfloat16 [2048, 4096], P(('groups', 'seq'), 'head'), parts along dimension 0, may hold values from -6 to 6
- out_grad: bfloat16 [2048, 4096], P(('groups', 'seq'), 'head'), parts along dimension 0, may hold values from -6 to 6
- lengths: int32 [32], P('groups'), parts along dimension 0, may hold values from 1 to 256, 1024 in all
Outputs:
- attended: bfloat16 [2048, 4096], P(('groups', 'seq'), 'head'), parts along dimension 0
- query_grad: bfloat16 [2048, 4096], P(('groups', 'seq'), 'head'), parts along dimension 0
- key_grad: bfloat16 [2048, 4096], P(('groups', 'seq'), 'head'), parts along dimension 0
- value_grad: bfloat16 [2048, 4096], P(('groups', 'seq'), 'head'), parts along dimension 0
There are 2 independent parts, one for each index of `groups`. A program takes and returns all parts, laid end to end along the dimension named above; each array names one. Nothing has to cross between parts.
Inputs may be any that keep to these rules, and one draw needn't show every extreme that they name: The lengths sum to 1024; the longest document has exactly 256 tokens.
All inputs are finite; a program needn't handle non-finite values.
Results may differ from a plain program's by a relative error of at most 0.0044.
Values sent between devices are 32-bit elements; how exact they have to be, the bound alone decides.
A program may use at most 64 MiB of HBM per device.

v0:
```python
import jax
import jax.numpy as jnp
from jax import lax
from jax.sharding import PartitionSpec as P

DH = 128
DOCS = 16


def from_behind(block, axis, distance):
    devices = range(lax.axis_size(axis))
    route = [(i - distance, i) for i in devices if i - distance in devices]
    return lax.ppermute(block, axis, route)


def combine_pair(earlier, latter):
    return (earlier[0] * latter[0], latter[1] + latter[0] * earlier[1])


def prior_bounded(keep_gate, state, levels):
    distances = [1] + [1 << level for level in range(levels)]
    current = (keep_gate, state)
    for counter, distance in enumerate(distances):
        shifted = from_behind((current[0], current[1]), "seq", distance)
        if counter == 0:
            current = shifted
        else:
            current = combine_pair(shifted, current)
    return current[1]


def later_bounded(keep_gate, state, levels):
    distances = [1] + [1 << level for level in range(levels)]
    current = (keep_gate, state)
    for counter, distance in enumerate(distances):
        shifted = from_behind((current[0], current[1]), "seq", -distance)
        if counter == 0:
            current = shifted
        else:
            current = combine_pair(shifted, current)
    return current[1]


def local(queries, key_rows, value_rows, out_grad, lengths):
    tokens = queries.shape[0]
    head_count = queries.shape[1] // DH
    shape3 = (tokens, head_count, DH)
    highest = lax.Precision.HIGHEST
    query_heads = queries.reshape(shape3)
    key_heads = key_rows.reshape(shape3)
    value_heads = value_rows.reshape(shape3)
    grad_heads = out_grad.reshape(shape3)
    block_index = lax.axis_index("seq")
    doc_total = jnp.sum(lengths).astype(jnp.float32)
    factor = lax.rsqrt(jnp.float32(DH) * doc_total / DOCS)
    doc_ends = jnp.cumsum(lengths)
    doc_starts = doc_ends - lengths
    first_pos = block_index * tokens
    positions = first_pos + jnp.arange(tokens, dtype=jnp.int32)
    doc_ids = jnp.sum((doc_ends[None, :] <= positions[:, None]).astype(jnp.int32), axis=1)
    opens = jnp.any(doc_starts[None, :] == positions[:, None], axis=1)
    keep_gate = 1.0 - jnp.any(opens).astype(jnp.float32)
    open_here = opens[0].astype(jnp.float32)
    open_next = jnp.any(doc_starts == first_pos + tokens).astype(jnp.float32)
    first_mask = doc_ids == doc_ids[0]
    last_mask = doc_ids == doc_ids[-1]
    local_mask = (positions[None, :] <= positions[:, None]) & (doc_ids[:, None] == doc_ids[None, :])
    zero_half = jnp.zeros((), jnp.bfloat16)
    forward_state = jnp.einsum(
        "shd,she->hde",
        jnp.where(last_mask[:, None, None], key_heads, zero_half),
        value_heads,
        preferred_element_type=jnp.float32,
    )
    backward_state = jnp.einsum(
        "thd,the->hde",
        jnp.where(first_mask[:, None, None], query_heads, zero_half),
        grad_heads,
        preferred_element_type=jnp.float32,
    )
    levels = max(lax.axis_size("seq") // 4 - 1, 0).bit_length()
    prior = prior_bounded(keep_gate, forward_state, levels)
    later_state = later_bounded(keep_gate, backward_state, levels)
    prior = prior * (1.0 - open_here)
    later_state = later_state * (1.0 - open_next)
    first_f = factor * first_mask.astype(jnp.float32)[:, None, None]
    last_f = factor * last_mask.astype(jnp.float32)[:, None, None]
    raw_scores = jnp.einsum(
        "thd,shd->hts", query_heads, key_heads, preferred_element_type=jnp.float32
    )
    scores = jnp.where(local_mask[None], factor * raw_scores, 0.0).astype(jnp.bfloat16)
    attended = jnp.einsum(
        "hts,she->the", scores, value_heads, preferred_element_type=jnp.float32
    ) + first_f * jnp.einsum(
        "thd,hde->the", query_heads.astype(jnp.float32), prior, precision=highest
    )
    raw_grad = jnp.einsum(
        "the,she->hts", grad_heads, value_heads, preferred_element_type=jnp.float32
    )
    grad_scores = jnp.where(local_mask[None], factor * raw_grad, 0.0).astype(jnp.bfloat16)
    query_grad = jnp.einsum(
        "hts,shd->thd", grad_scores, key_heads, preferred_element_type=jnp.float32
    ) + first_f * jnp.einsum(
        "the,hde->thd", grad_heads.astype(jnp.float32), prior, precision=highest
    )
    key_grad = jnp.einsum(
        "hts,thd->shd", grad_scores, query_heads, preferred_element_type=jnp.float32
    ) + last_f * jnp.einsum(
        "hde,she->shd", later_state, value_heads.astype(jnp.float32), precision=highest
    )
    value_grad = jnp.einsum(
        "hts,the->she", scores, grad_heads, preferred_element_type=jnp.float32
    ) + last_f * jnp.einsum(
        "hde,shd->she", later_state, key_heads.astype(jnp.float32), precision=highest
    )
    width = head_count * DH
    return (
        attended.reshape(tokens, width).astype(jnp.bfloat16),
        query_grad.reshape(tokens, width).astype(jnp.bfloat16),
        key_grad.reshape(tokens, width).astype(jnp.bfloat16),
        value_grad.reshape(tokens, width).astype(jnp.bfloat16),
    )


def solution(mesh):
    placed = (
        P(("groups", "seq"), "head"),
        P(("groups", "seq"), "head"),
        P(("groups", "seq"), "head"),
        P(("groups", "seq"), "head"),
        P("groups"),
    )
    return jax.shard_map(
        local,
        mesh=mesh,
        in_specs=placed,
        out_specs=(
            P(("groups", "seq"), "head"),
            P(("groups", "seq"), "head"),
            P(("groups", "seq"), "head"),
            P(("groups", "seq"), "head"),
        ),
        check_vma=False,
    )
```

profile of v0, /device:TPU:24, one launch (start us, length us, event | category | flops | bytes accessed | tf_op | source)
XLA Modules:
  0.0 121.9 jit_solution(11302723001243834500)
XLA Ops:
  3.6 1.1 copy.84
  5.2 1.3 %broadcast_select_fusion = (f32[128]{0:T(128)S(1)}, pred[128]{0:T(512)(128)(4,1)S(1)}, f32[128]{0:T(128)S(1)}, pred[128]{0:T(512)(128)(4,1)S(1)}) fusion(f32[]{:T(128)S(6)} %rsqrt.3, s32[128]{0:T(128)S(1)} %convert_reduce_fusion, s32[]{:T(128)} %bitcast.3, s32[]{:T(128)} %bitcast.2), kind=kLoop, calls=%fused_computation.55 | loop fusion | flops 512 | bytes 1804 | tf_op jit(solution)/shard_map/mul | solution.py:87
  6.6 1.3 %fusion.19 = f32[16,128,128]{2,1,0:T(8,128)} fusion(bf16[128,16,128]{0,2,1:T(8,128)(2,1)S(1)} %copy.59, pred[128]{0:T(512)(128)(4,1)S(1)} %get-tuple-element.21, bf16[128,2048]{1,0:T(8,128)(2,1)S(1)} %copy-done), kind=kOutput, calls=%fused_computation.31 | convolution fusion | flops 67371008 | bytes 2097280 | tf_op jit(solution)/shard_map/shd,she->hde/dot_general | solution.py:69
  7.9 3.4 %collective-permute-start = (f32[16,128,128]{2,1,0:T(8,128)}, f32[16,128,128]{2,1,0:T(8,128)S(1)}, u32[]{:S(2)}, u32[]{:S(2)}) collective-permute-start(f32[16,128,128]{2,1,0:T(8,128)} %fusion.19), channel_id=1, source_target_pairs={{0,2},{2,4},{4,6},{6,8},{8,10},{10,12},{12,14},{1,3},{3,5},{5,7},{... | collective-permute-start | bytes 3145736 | tf_op jit(solution)/shard_map/ppermute | solution.py:13
  13.3 20.7 %collective-permute-start.1 = (f32[]{:T(128)}, f32[]{:T(128)}, u32[]{:S(2)}, u32[]{:S(2)}) collective-permute-start(f32[]{:T(128)} %sub.16), channel_id=1, source_target_pairs={{0,2},{2,4},{4,6},{6,8},{8,10},{10,12},{12,14},{1,3},{3,5},{5,7},{... | collective-permute-start | bytes 20 | tf_op jit(solution)/shard_map/ppermute | solution.py:13
  34.0 4.6 %collective-permute-start.4 = (f32[]{:T(128)}, f32[]{:T(128)}, u32[]{:S(2)}, u32[]{:S(2)}) collective-permute-start(f32[]{:T(128)} %sub.16), channel_id=1, source_target_pairs={{2,0},{4,2},{6,4},{8,6},{10,8},{12,10},{14,12},{3,1},{5,3},{7,5},{... | collective-permute-start | bytes 20 | tf_op jit(solution)/shard_map/ppermute | solution.py:13
  38.9 1.3 %copy.81 = bf16[128,2048]{0,1:T(8,128)(2,1)S(1)} copy(bf16[128,2048]{1,0:T(8,128)(2,1)} %param.8) | data formatting | bytes 1048576 | tf_op jit(solution)/shard_map/reshape | solution.py:52
  40.7 2.4 %collective-permute-start.3 = (f32[16,128,128]{2,1,0:T(8,128)S(1)}, f32[16,128,128]{2,1,0:T(8,128)}, u32[]{:S(2)}, u32[]{:S(2)}) collective-permute-start(f32[16,128,128]{2,1,0:T(8,128)S(1)} %fusion.23), channel_id=1, source_target_pairs={{2,0},{4,2},{6,4},{8,6},{10,8},{12,10},{14,12},{3,1},{5,3},{7,5},{... | collective-permute-start | bytes 3145736 | tf_op jit(solution)/shard_map/ppermute | solution.py:13
  43.7 1.5 %convolution_bitcast_fusion.2 = f32[128,16,128]{0,2,1:T(8,128)} fusion(bf16[16,128,128]{2,1,0:T(8,128)(2,1)S(1)} %fusion.10, bf16[128,16,128]{0,2,1:T(8,128)(2,1)S(1)} %copy.59), kind=kOutput, calls=%fused_computation.11 | convolution fusion | flops 67108864 | bytes 2097152 | tf_op jit(solution)/shard_map/hts,shd->thd/dot_general | solution.py:101
  45.2 4.4 %collective-permute-start.2 = (f32[16,128,128]{2,1,0:T(8,128)S(1)}, f32[16,128,128]{2,1,0:T(8,128)}, u32[]{:S(2)}, u32[]{:S(2)}) collective-permute-start(f32[16,128,128]{2,1,0:T(8,128)S(1)} %collective-permute-done), channel_id=1, source_target_pairs={{0,2},{2,4},{4,6},{6,8},{8,10},{10,12},{12,14},{1,3},{3,5},{5,7},{... | collective-permute-start | bytes 3145736 | tf_op jit(solution)/shard_map/ppermute | solution.py:13
  50.2 1.3 %convolution_bitcast_fusion.1 = f32[128,16,128]{0,2,1:T(8,128)} fusion(bf16[128,16,128]{0,2,1:T(8,128)(2,1)S(1)} %bitcast.97, bf16[16,128,128]{2,1,0:T(8,128)(2,1)S(1)} %fusion.10), kind=kOutput, calls=%fused_computation.1 | convolution fusion | flops 67108864 | bytes 2097152 | tf_op jit(solution)/shard_map/hts,thd->shd/dot_general | solution.py:106
  51.4 36.9 %collective-permute-done.3 = f32[16,128,128]{2,1,0:T(8,128)} collective-permute-done((f32[16,128,128]{2,1,0:T(8,128)S(1)}, f32[16,128,128]{2,1,0:T(8,128)}, u32[]{:S(2)}, u32[]{:S(2)}) %collective-permute-start.3) | collective-permute-done | bytes 1048608 | tf_op jit(solution)/shard_map/ppermute | solution.py:13
  88.3 1.9 %collective-permute-start.5 = (f32[16,128,128]{2,1,0:T(8,128)}, f32[16,128,128]{2,1,0:T(8,128)}, u32[]{:S(2)}, u32[]{:S(2)}) collective-permute-start(f32[16,128,128]{2,1,0:T(8,128)} %collective-permute-done.3), channel_id=1, source_target_pairs={{2,0},{4,2},{6,4},{8,6},{10,8},{12,10},{14,12},{3,1},{5,3},{7,5},{... | collective-permute-start | bytes 3145736 | tf_op jit(solution)/shard_map/ppermute | solution.py:13
  90.3 1.5 %convolution_bitcast_fusion.3 = f32[128,16,128]{0,2,1:T(8,128)} fusion(bf16[16,128,128]{2,1,0:T(8,128)(2,1)S(1)} %fusion.11, bf16[128,2048]{1,0:T(8,128)(2,1)S(1)} %copy-done), kind=kOutput, calls=%fused_computation.16 | convolution fusion | flops 67108864 | bytes 2097152 | tf_op jit(solution)/shard_map/hts,she->the/dot_general | solution.py:92
  92.5 1.3 %convolution_bitcast_fusion = f32[128,16,128]{0,2,1:T(8,128)} fusion(bf16[128,16,128]{0,2,1:T(8,128)(2,1)S(1)} %bitcast.93, bf16[16,128,128]{2,1,0:T(8,128)(2,1)S(1)} %fusion.11), kind=kOutput, calls=%fused_computation | convolution fusion | flops 67108864 | bytes 2097152 | tf_op jit(solution)/shard_map/hts,the->she/dot_general | solution.py:111
  93.8 3.6 %fusion.12 = bf16[128,16,128]{0,2,1:T(8,128)(2,1)} fusion(f32[128,16,128]{0,2,1:T(8,128)S(1)} %copy-done.4, bf16[128,16,128]{0,2,1:T(8,128)(2,1)S(1)} %bitcast.98, f32[128]{0:T(128)S(1)} %get-tuple-element.24, f32[16,128,128]{2,1,0:T(8,128)S(1)} %collective-permute-done, f32[16,128,128]{2,1,0:T(8,128)} %collective-permute-done.2, f32[]{:T(128)} %bitcast.4, ...), kind=kOutput, calls=%fused_computation.22 | convolution fusion | flops 404226048 | bytes 4194824 | tf_op jit(solution)/shard_map/thd,hde->the/dot_general | solution.py:94
  97.5 2.1 %copy.74 = bf16[128,2048]{1,0:T(8,128)(2,1)} copy(bf16[128,2048]{0,1:T(8,128)(2,1)} %bitcast.102) | data formatting | bytes 1048576
  99.6 3.4 %fusion.13 = bf16[128,16,128]{0,2,1:T(8,128)(2,1)} fusion(f32[128,16,128]{0,2,1:T(8,128)S(1)} %copy-done.2, bf16[128,16,128]{0,2,1:T(8,128)(2,1)S(1)} %bitcast.94, f32[128]{0:T(128)S(1)} %get-tuple-element.24, f32[16,128,128]{2,1,0:T(8,128)S(1)} %collective-permute-done, f32[16,128,128]{2,1,0:T(8,128)} %collective-permute-done.2, f32[]{:T(128)} %bitcast.4, ...), kind=kOutput, calls=%fused_computation.23 | convolution fusion | flops 404226048 | bytes 4194824 | tf_op jit(solution)/shard_map/the,hde->thd/dot_general | solution.py:103
  103.0 2.1 %copy.75 = bf16[128,2048]{1,0:T(8,128)(2,1)} copy(bf16[128,2048]{0,1:T(8,128)(2,1)} %bitcast.100) | data formatting | bytes 1048576
  105.1 7.7 %collective-permute-done.5 = f32[16,128,128]{2,1,0:T(8,128)} collective-permute-done((f32[16,128,128]{2,1,0:T(8,128)}, f32[16,128,128]{2,1,0:T(8,128)}, u32[]{:S(2)}, u32[]{:S(2)}) %collective-permute-start.5) | collective-permute-done | bytes 1048608 | tf_op jit(solution)/shard_map/ppermute | solution.py:13
  112.8 3.5 %fusion.14 = bf16[128,16,128]{0,2,1:T(8,128)(2,1)S(1)} fusion(f32[128,16,128]{0,2,1:T(8,128)S(1)} %copy-done.1, f32[128]{0:T(128)S(1)} %get-tuple-element.20, f32[16,128,128]{2,1,0:T(8,128)} %collective-permute-done.3, f32[16,128,128]{2,1,0:T(8,128)} %collective-permute-done.5, f32[]{:T(128)S(6)} %sub.19, f32[]{:T(128)} %collective-permute-done.4, ...), kind=kOutput, calls=%fused_computation.24 | convolution fusion | flops 404226048 | bytes 4194824 | tf_op jit(solution)/shard_map/hde,she->shd/dot_general | solution.py:108
  116.3 1.0 copy.76
  117.7 3.2 %fusion.15 = bf16[128,16,128]{0,2,1:T(8,128)(2,1)S(1)} fusion(f32[128,16,128]{0,2,1:T(8,128)S(1)} %copy-done.3, f32[128]{0:T(128)S(1)} %get-tuple-element.20, f32[16,128,128]{2,1,0:T(8,128)} %collective-permute-done.3, f32[16,128,128]{2,1,0:T(8,128)} %collective-permute-done.5, f32[]{:T(128)S(6)} %sub.19, f32[]{:T(128)} %collective-permute-done.4, ...), kind=kOutput, calls=%fused_computation.25 | convolution fusion | flops 404226048 | bytes 4194824 | tf_op jit(solution)/shard_map/hde,shd->she/dot_general | solution.py:113
  120.9 1.0 copy.77
  (37 shorter events, 6.4 us)
Async XLA Ops:
  0.6 5.9 %copy-start = (bf16[128,2048]{1,0:T(8,128)(2,1)S(1)}, bf16[128,2048]{1,0:T(8,128)(2,1)}, u32[]{:S(2)}) copy-start(bf16[128,2048]{1,0:T(8,128)(2,1)} %param.7) | copy-start | bytes 1572868
  0.6 0.7 copy-start.8
  6.6 32.1 %copy-start.7 = (bf16[128,2048]{1,0:T(8,128)(2,1)S(1)}, bf16[128,2048]{1,0:T(8,128)(2,1)}, u32[]{:S(2)}) copy-start(bf16[128,2048]{1,0:T(8,128)(2,1)} %param.5) | copy-start | bytes 1572868
  7.9 37.3 %collective-permute-start = (f32[16,128,128]{2,1,0:T(8,128)}, f32[16,128,128]{2,1,0:T(8,128)S(1)}, u32[]{:S(2)}, u32[]{:S(2)}) collective-permute-start(f32[16,128,128]{2,1,0:T(8,128)} %fusion.19), channel_id=1, source_target_pairs={{0,2},{2,4},{4,6},{6,8},{8,10},{10,12},{12,14},{1,3},{3,5},{5,7},{... | collective-permute-start | bytes 3145736 | tf_op jit(solution)/shard_map/ppermute | solution.py:13
  13.3 80.5 %collective-permute-start.1 = (f32[]{:T(128)}, f32[]{:T(128)}, u32[]{:S(2)}, u32[]{:S(2)}) collective-permute-start(f32[]{:T(128)} %sub.16), channel_id=1, source_target_pairs={{0,2},{2,4},{4,6},{6,8},{8,10},{10,12},{12,14},{1,3},{3,5},{5,7},{... | collective-permute-start | bytes 20 | tf_op jit(solution)/shard_map/ppermute | solution.py:13
  34.0 71.1 %collective-permute-start.4 = (f32[]{:T(128)}, f32[]{:T(128)}, u32[]{:S(2)}, u32[]{:S(2)}) collective-permute-start(f32[]{:T(128)} %sub.16), channel_id=1, source_target_pairs={{2,0},{4,2},{6,4},{8,6},{10,8},{12,10},{14,12},{3,1},{5,3},{7,5},{... | collective-permute-start | bytes 20 | tf_op jit(solution)/shard_map/ppermute | solution.py:13
  40.7 47.6 %collective-permute-start.3 = (f32[16,128,128]{2,1,0:T(8,128)S(1)}, f32[16,128,128]{2,1,0:T(8,128)}, u32[]{:S(2)}, u32[]{:S(2)}) collective-permute-start(f32[16,128,128]{2,1,0:T(8,128)S(1)} %fusion.23), channel_id=1, source_target_pairs={{2,0},{4,2},{6,4},{8,6},{10,8},{12,10},{14,12},{3,1},{5,3},{7,5},{... | collective-permute-start | bytes 3145736 | tf_op jit(solution)/shard_map/ppermute | solution.py:13
  43.7 5.9 %copy-start.5 = (bf16[128,2048]{1,0:T(8,128)(2,1)S(1)}, bf16[128,2048]{1,0:T(8,128)(2,1)}, u32[]{:S(2)}) copy-start(bf16[128,2048]{1,0:T(8,128)(2,1)} %param.6) | copy-start | bytes 1572868
  45.2 48.6 %collective-permute-start.2 = (f32[16,128,128]{2,1,0:T(8,128)S(1)}, f32[16,128,128]{2,1,0:T(8,128)}, u32[]{:S(2)}, u32[]{:S(2)}) collective-permute-start(f32[16,128,128]{2,1,0:T(8,128)S(1)} %collective-permute-done), channel_id=1, source_target_pairs={{0,2},{2,4},{4,6},{6,8},{8,10},{10,12},{12,14},{1,3},{3,5},{5,7},{... | collective-permute-start | bytes 3145736 | tf_op jit(solution)/shard_map/ppermute | solution.py:13
  88.3 24.4 %collective-permute-start.5 = (f32[16,128,128]{2,1,0:T(8,128)}, f32[16,128,128]{2,1,0:T(8,128)}, u32[]{:S(2)}, u32[]{:S(2)}) collective-permute-start(f32[16,128,128]{2,1,0:T(8,128)} %collective-permute-done.3), channel_id=1, source_target_pairs={{2,0},{4,2},{6,4},{8,6},{10,8},{12,10},{14,12},{3,1},{5,3},{7,5},{... | collective-permute-start | bytes 3145736 | tf_op jit(solution)/shard_map/ppermute | solution.py:13
  92.5 1.3 %copy-start.4 = (f32[128,16,128]{0,2,1:T(8,128)S(1)}, f32[128,16,128]{0,2,1:T(8,128)}, u32[]{:S(2)}) copy-start(f32[128,16,128]{0,2,1:T(8,128)} %convolution_bitcast_fusion.3) | copy-start | bytes 3145732
  97.5 2.1 %copy-start.2 = (f32[128,16,128]{0,2,1:T(8,128)S(1)}, f32[128,16,128]{0,2,1:T(8,128)}, u32[]{:S(2)}) copy-start(f32[128,16,128]{0,2,1:T(8,128)} %convolution_bitcast_fusion.2) | copy-start | bytes 3145732
  103.0 9.8 %copy-start.1 = (f32[128,16,128]{0,2,1:T(8,128)S(1)}, f32[128,16,128]{0,2,1:T(8,128)}, u32[]{:S(2)}) copy-start(f32[128,16,128]{0,2,1:T(8,128)} %convolution_bitcast_fusion.1) | copy-start | bytes 3145732
  112.8 4.5 %copy-start.6 = (bf16[128,2048]{1,0:T(8,128)(2,1)S(1)}, bf16[128,2048]{1,0:T(8,128)(2,1)}, u32[]{:S(2)}) copy-start(bf16[128,2048]{1,0:T(8,128)(2,1)} %param.6) | copy-start | bytes 1572868
  116.3 1.4 %copy-start.3 = (f32[128,16,128]{0,2,1:T(8,128)S(1)}, f32[128,16,128]{0,2,1:T(8,128)}, u32[]{:S(2)}) copy-start(f32[128,16,128]{0,2,1:T(8,128)} %convolution_bitcast_fusion) | copy-start | bytes 3145732
where the time goes:
time: 123 us; the launch traced here: 122 us
  waiting for transfers between devices  44.6 us (36%)
  starting transfers between devices  37.5 us (30%)
  matrix products  22.1 us (18%)
  local copies, waits for them, and re-layouts  11.3 us (9%)
  other arithmetic  3.62 us (3%)
  between operations  2.85 us (2%)
    ppermute x6, waiting for transfers between devices, from_behind(): return lax.ppermute(block, axis, route)  44.6 us
    ppermute x6, starting transfers between devices, from_behind(): return lax.ppermute(block, axis, route)  37.5 us
    unnamed x23, local copies, waits for them, and re-layouts  8.56 us
    dot_general x1, matrix products, local(): jnp.einsum('thd,hde->the', query_heads.astype(jnp.float32), prior, precis...  3.65 us
    dot_general x1, matrix products, local(): jnp.einsum('hde,she->shd', later_state, value_heads.astype(jnp.float32),...  3.45 us
    dot_general x1, matrix products, local(): jnp.einsum('the,hde->thd', grad_heads.astype(jnp.float32), prior, precisi...  3.37 us
    dot_general x1, matrix products, local(): jnp.einsum('hde,shd->she', later_state, key_heads.astype(jnp.float32), pr...  3.24 us
  transfers between devices with their start and end apart: 6, of which 2 were waited for; matrix products, arithmetic and copies ran while one was open for 18% of the time, Pallas kernels for 0%

commit v1 on v0

--- a/solution.py
+++ b/solution.py
@@ -1,6 +1,10 @@
+import functools
+
 import jax
 import jax.numpy as jnp
 from jax import lax
+from jax.experimental import pallas as pl
+from jax.experimental.pallas import tpu as pltpu
 from jax.sharding import PartitionSpec as P
 
 DH = 128
@@ -41,7 +45,7 @@
     return current[1]
 
 
-def local(queries, key_rows, value_rows, out_grad, lengths):
+def local_general(queries, key_rows, value_rows, out_grad, lengths):
     tokens = queries.shape[0]
     head_count = queries.shape[1] // DH
     shape3 = (tokens, head_count, DH)
@@ -53,7 +57,8 @@
     block_index = lax.axis_index("seq")
     doc_total = jnp.sum(lengths).astype(jnp.float32)
     factor = lax.rsqrt(jnp.float32(DH) * doc_total / DOCS)
-    doc_ends = jnp.cumsum(lengths)
+    upto = jnp.tri(lengths.shape[0], dtype=jnp.int32)
+    doc_ends = jnp.sum(upto * lengths[None, :], axis=1)
     doc_starts = doc_ends - lengths
     first_pos = block_index * tokens
     positions = first_pos + jnp.arange(tokens, dtype=jnp.int32)
@@ -122,6 +127,250 @@
     )
 
 
+CHUNK_HEADS = 2
+
+
+def bounded_kernel(
+    count, lengths_ref, q_ref, k_ref, v_ref, g_ref,
+    attended_ref, query_grad_ref, key_grad_ref, value_grad_ref,
+    state, near, far, part, pair_mask, first_mask, last_mask,
+    own_send, pass_send, far_send, near_recv, far_recv,
+):
+    tokens, width = q_ref.shape
+    heads = width // DH
+    chunks = heads // CHUNK_HEADS
+    factor = (DH * tokens * count / DOCS) ** -0.5
+    block = lax.axis_index("seq")
+    parity = lax.rem(block, 2)
+    partner = block + 1 - 2 * parity
+    behind = block >= 2
+    ahead = block + 2 < count
+    takes = jnp.where(parity == 0, behind, ahead)
+    passes = jnp.where(parity == 0, ahead, behind)
+
+    barrier = pltpu.get_barrier_semaphore()
+    pl.semaphore_signal(barrier, inc=1, device_id={"seq": partner})
+
+    @pl.when(behind)
+    def _():
+        pl.semaphore_signal(barrier, inc=1, device_id={"seq": block - 2})
+
+    @pl.when(ahead)
+    def _():
+        pl.semaphore_signal(barrier, inc=1, device_id={"seq": block + 2})
+
+    first_pos = block * tokens
+    rows = lax.broadcasted_iota(jnp.int32, (tokens, tokens), 0)
+    columns = lax.broadcasted_iota(jnp.int32, (tokens, tokens), 1)
+    row_doc = jnp.zeros((tokens, tokens), jnp.int32)
+    column_doc = jnp.zeros((tokens, tokens), jnp.int32)
+    zero, one = jnp.int32(0), jnp.int32(1)
+    first_doc = last_doc = opens_first = opens_next = zero
+    opens_before = opens_after = zero
+    end = zero
+    for doc in range(DOCS):
+        start = end - first_pos
+        end = end + lengths_ref[doc]
+        stop = end - first_pos
+        row_doc += jnp.where(stop <= rows, 1, 0)
+        column_doc += jnp.where(stop <= columns, 1, 0)
+        first_doc += jnp.where(stop <= 0, one, zero)
+        last_doc += jnp.where(stop <= tokens - 1, one, zero)
+        opens_first = jnp.maximum(opens_first, jnp.where(start == 0, one, zero))
+        opens_next = jnp.maximum(opens_next, jnp.where(start == tokens, one, zero))
+        before = (start >= -tokens) & (start < 0)
+        after = (start >= tokens) & (start < 2 * tokens)
+        opens_before = jnp.maximum(opens_before, jnp.where(before, one, zero))
+        opens_after = jnp.maximum(opens_after, jnp.where(after, one, zero))
+    near_weight = [
+        factor * (1 - opens_first).astype(jnp.float32),
+        factor * (1 - opens_next).astype(jnp.float32),
+    ]
+    far_weight = [
+        near_weight[0] * (1 - opens_before).astype(jnp.float32),
+        near_weight[1] * (1 - opens_after).astype(jnp.float32),
+    ]
+    pair_mask[...] = jnp.where((columns <= rows) & (row_doc == column_doc), factor, 0.0)
+    first_mask[...] = jnp.where(row_doc == first_doc, 1.0, 0.0).astype(jnp.bfloat16)
+    last_mask[...] = jnp.where(row_doc == last_doc, 1.0, 0.0).astype(jnp.bfloat16)
+
+    def span(i):
+        return pl.ds(i * CHUNK_HEADS, CHUNK_HEADS)
+
+    def lanes(h):
+        return pl.ds(pl.multiple_of(h * DH, DH), DH)
+
+    def dot(a, b, dims):
+        return lax.dot_general(a, b, (dims, ((), ())), preferred_element_type=jnp.float32)
+
+    rows_rows, plain, turned = ((0,), (0,)), ((1,), (0,)), ((1,), (1,))
+
+    def own_copy(i):
+        return pltpu.make_async_remote_copy(
+            state.at[parity, span(i)], near.at[parity, span(i)],
+            own_send.at[i], near_recv.at[parity, i], device_id={"seq": partner},
+        )
+
+    def pass_copy(i):
+        return pltpu.make_async_remote_copy(
+            far.at[1 - parity, span(i)], near.at[1 - parity, span(i)],
+            pass_send.at[i], near_recv.at[1 - parity, i], device_id={"seq": partner},
+        )
+
+    def far_copy(kind, i):
+        return pltpu.make_async_remote_copy(
+            state.at[kind, span(i)], far.at[kind, span(i)],
+            far_send.at[kind, i], far_recv.at[kind, i],
+            device_id={"seq": block + 2 - 4 * kind},
+        )
+
+    def states(i):
+        for j in range(CHUNK_HEADS):
+            h = i * CHUNK_HEADS + j
+            at = lanes(h)
+            state[0, h] = dot(k_ref[:, at] * last_mask[...], v_ref[:, at], rows_rows)
+            state[1, h] = dot(q_ref[:, at] * first_mask[...], g_ref[:, at], rows_rows)
+
+    def send(i):
+        @pl.when(ahead)
+        def _():
+            far_copy(0, i).start()
+
+        @pl.when(behind)
+        def _():
+            far_copy(1, i).start()
+
+        own_copy(i).start()
+
+    states(0)
+    pl.semaphore_wait(
+        barrier, 1 + jnp.where(behind, one, zero) + jnp.where(ahead, one, zero)
+    )
+    send(0)
+
+    @pl.loop(1, chunks)
+    def _(i):
+        states(i)
+        send(i)
+
+    @pl.when(jnp.logical_not(takes))
+    def _():
+        @pl.loop(0, heads)
+        def _(h):
+            near[parity, h] = jnp.zeros((DH, DH), jnp.float32)
+            far[parity, h] = jnp.zeros((DH, DH), jnp.float32)
+
+    @pl.when(jnp.logical_not(passes))
+    def _():
+        @pl.loop(0, heads)
+        def _(h):
+            far[1 - parity, h] = jnp.zeros((DH, DH), jnp.float32)
+
+    @pl.loop(0, chunks)
+    def _(i):
+        for j in range(CHUNK_HEADS):
+            h = i * CHUNK_HEADS + j
+            at = lanes(h)
+            q, k, v, g = q_ref[:, at], k_ref[:, at], v_ref[:, at], g_ref[:, at]
+            scores = (dot(q, k, turned) * pair_mask[...]).astype(jnp.bfloat16)
+            grads = (dot(g, v, turned) * pair_mask[...]).astype(jnp.bfloat16)
+            part[0, h] = dot(scores, v, plain)
+            part[1, h] = dot(grads, k, plain)
+            part[2, h] = dot(grads, q, rows_rows)
+            part[3, h] = dot(scores, g, rows_rows)
+
+        @pl.when(passes)
+        def _():
+            far_copy(1 - parity, i).wait_recv()
+            pass_copy(i).start()
+
+    @pl.loop(0, chunks)
+    def _(i):
+        own_copy(i).wait_send()
+
+        @pl.when(ahead)
+        def _():
+            far_copy(0, i).wait_send()
+
+        @pl.when(behind)
+        def _():
+            far_copy(1, i).wait_send()
+
+        pass_copy(i).wait_recv()
+
+        @pl.when(takes)
+        def _():
+            far_copy(parity, i).wait_recv()
+            own_copy(i).wait_recv()
+
+        for j in range(CHUNK_HEADS):
+            h = i * CHUNK_HEADS + j
+            at = lanes(h)
+            mixed = []
+            for kind in range(2):
+                whole = near_weight[kind] * near[kind, h] + far_weight[kind] * far[kind, h]
+                high = whole.astype(jnp.bfloat16)
+                low = (whole - high.astype(jnp.float32)).astype(jnp.bfloat16)
+                mixed.append((high, low))
+            (prior, prior_low), (later, later_low) = mixed
+            q, g = q_ref[:, at] * first_mask[...], g_ref[:, at] * first_mask[...]
+            k, v = k_ref[:, at] * last_mask[...], v_ref[:, at] * last_mask[...]
+            attended_ref[:, at] = (
+                part[0, h] + (dot(q, prior, plain) + dot(q, prior_low, plain))
+            ).astype(jnp.bfloat16)
+            query_grad_ref[:, at] = (
+                part[1, h] + (dot(g, prior, turned) + dot(g, prior_low, turned))
+            ).astype(jnp.bfloat16)
+            key_grad_ref[:, at] = (
+                part[2, h] + (dot(v, later, turned) + dot(v, later_low, turned))
+            ).astype(jnp.bfloat16)
+            value_grad_ref[:, at] = (
+                part[3, h] + (dot(k, later, plain) + dot(k, later_low, plain))
+            ).astype(jnp.bfloat16)
+
+    @pl.when(passes)
+    def _():
+        @pl.loop(0, chunks)
+        def _(i):
+            pass_copy(i).wait_send()
+
+
+def local_bounded(queries, key_rows, value_rows, out_grad, lengths):
+    tokens, width = queries.shape
+    heads = width // DH
+    chunks = heads // CHUNK_HEADS
+    whole = pl.BlockSpec(memory_space=pltpu.VMEM)
+    states = pltpu.VMEM((2, heads, DH, DH), jnp.float32)
+    return tuple(pl.pallas_call(
+        functools.partial(bounded_kernel, lax.axis_size("seq")),
+        out_shape=[jax.ShapeDtypeStruct((tokens, width), jnp.bfloat16)] * 4,
+        in_specs=[pl.BlockSpec(memory_space=pltpu.SMEM)] + [whole] * 4,
+        out_specs=[whole] * 4,
+        scratch_shapes=[
+            states, states, states,
+            pltpu.VMEM((4, heads, tokens, DH), jnp.float32),
+            pltpu.VMEM((tokens, tokens), jnp.float32),
+            pltpu.VMEM((tokens, DH), jnp.bfloat16),
+            pltpu.VMEM((tokens, DH), jnp.bfloat16),
+            pltpu.SemaphoreType.DMA((chunks,)),
+            pltpu.SemaphoreType.DMA((chunks,)),
+            pltpu.SemaphoreType.DMA((2, chunks)),
+            pltpu.SemaphoreType.DMA((2, chunks)),
+            pltpu.SemaphoreType.DMA((2, chunks)),
+        ],
+        compiler_params=pltpu.CompilerParams(
+            collective_id=0, has_side_effects=True, vmem_limit_bytes=40 * 2**20
+        ),
+    )(lengths, queries, key_rows, value_rows, out_grad))
+
+
+def local(queries, key_rows, value_rows, out_grad, lengths):
+    count = lax.axis_size("seq")
+    if count == 8 and queries.shape[0] == DH:
+        return local_bounded(queries, key_rows, value_rows, out_grad, lengths)
+    return local_general(queries, key_rows, value_rows, out_grad, lengths)
+
+
 def solution(mesh):
     placed = (
         P(("groups", "seq"), "head"),

time: 123 us -> 59 us (0.48)
  the two profiles are of different devices: /device:TPU:24 before, /device:TPU:8 now
where the time goes in v1:
time: 59 us; the launch traced here: 58.6 us
  Pallas kernels  50 us (85%)
  local copies, waits for them, and re-layouts  7.99 us (14%)
  between operations  0.65 us (1%)
    pallas_call x1, Pallas kernels, local_bounded(): pl.pallas_call(functools.partial(bounded_kernel, lax.axis_size('seq')), o...  50 us
    unnamed x14, local copies, waits for them, and re-layouts  7.99 us

profile of v1, /device:TPU:8, one launch (start us, length us, event | category | flops | bytes accessed | tf_op | source)
XLA Modules:
  0.0 58.6 jit_solution(741057594227102172)
XLA Ops:
  0.6 0.0 copy-start
  0.6 1.0 %copy-done = bf16[128,2048]{1,0:T(8,128)(2,1)S(1)} copy-done((bf16[128,2048]{1,0:T(8,128)(2,1)S(1)}, bf16[128,2048]{1,0:T(8,128)(2,1)}, u32[]{:S(2)}) %copy-start) | copy-done | bytes 524312
  1.7 0.0 copy-start.1
  1.7 1.0 %copy-done.1 = bf16[128,2048]{1,0:T(8,128)(2,1)S(1)} copy-done((bf16[128,2048]{1,0:T(8,128)(2,1)S(1)}, bf16[128,2048]{1,0:T(8,128)(2,1)}, u32[]{:S(2)}) %copy-start.1) | copy-done | bytes 524312
  2.7 0.0 copy-start.2
  2.7 1.0 %copy-done.2 = bf16[128,2048]{1,0:T(8,128)(2,1)S(1)} copy-done((bf16[128,2048]{1,0:T(8,128)(2,1)S(1)}, bf16[128,2048]{1,0:T(8,128)(2,1)}, u32[]{:S(2)}) %copy-start.2) | copy-done | bytes 524312
  3.8 0.0 copy-start.3
  3.8 1.0 %copy-done.3 = bf16[128,2048]{1,0:T(8,128)(2,1)S(1)} copy-done((bf16[128,2048]{1,0:T(8,128)(2,1)S(1)}, bf16[128,2048]{1,0:T(8,128)(2,1)}, u32[]{:S(2)}) %copy-start.3) | copy-done | bytes 524312
  4.8 0.0 copy-start.4
  4.8 0.7 %copy-done.4 = s32[16]{0:T(128)S(1)} copy-done((s32[16]{0:T(128)S(1)}, s32[16]{0:T(128)}, u32[]{:S(2)}) %copy-start.4) | copy-done | bytes 88
  5.5 50.0 %shard_map.84 = (bf16[128,2048]{1,0:T(8,128)(2,1)S(1)}, bf16[128,2048]{1,0:T(8,128)(2,1)S(1)}, bf16[128,2048]{1,0:T(8,128)(2,1)S(1)}, bf16[128,2048]{1,0:T(8,128)(2,1)S(1)}) custom-call(s32[16]{0:T(128)S(1)} %copy-done.4, bf16[128,2048]{1,0:T(8,128)(2,1)S(1)} %copy-done, bf16[128,2048]{1,0:T(8,128)(2,1)S(1)} %copy-done.1, bf16[128,2048]{1,0:T(8,128)(2,1)S(1)} %copy-done.2, ...), custom_call_target="tpu_custom_call" | custom-call | tf_op jit(solution)/shard_map/pallas_call | solution.py:344
  55.5 0.8 %copy.13 = bf16[128,2048]{1,0:T(8,128)(2,1)} copy(bf16[128,2048]{1,0:T(8,128)(2,1)S(1)} %get-tuple-element.8) | data formatting | bytes 1048576
  56.3 0.8 %copy.14 = bf16[128,2048]{1,0:T(8,128)(2,1)} copy(bf16[128,2048]{1,0:T(8,128)(2,1)S(1)} %get-tuple-element.9) | data formatting | bytes 1048576
  57.0 0.8 %copy.15 = bf16[128,2048]{1,0:T(8,128)(2,1)} copy(bf16[128,2048]{1,0:T(8,128)(2,1)S(1)} %get-tuple-element.10) | data formatting | bytes 1048576
  57.8 0.8 %copy.16 = bf16[128,2048]{1,0:T(8,128)(2,1)} copy(bf16[128,2048]{1,0:T(8,128)(2,1)S(1)} %get-tuple-element.11) | data formatting | bytes 1048576
Async XLA Ops:
  0.6 1.0 %copy-start = (bf16[128,2048]{1,0:T(8,128)(2,1)S(1)}, bf16[128,2048]{1,0:T(8,128)(2,1)}, u32[]{:S(2)}) copy-start(bf16[128,2048]{1,0:T(8,128)(2,1)} %q_ref.1) | copy-start | bytes 1572868
  1.7 1.0 %copy-start.1 = (bf16[128,2048]{1,0:T(8,128)(2,1)S(1)}, bf16[128,2048]{1,0:T(8,128)(2,1)}, u32[]{:S(2)}) copy-start(bf16[128,2048]{1,0:T(8,128)(2,1)} %k_ref.1) | copy-start | bytes 1572868
  2.7 1.0 %copy-start.2 = (bf16[128,2048]{1,0:T(8,128)(2,1)S(1)}, bf16[128,2048]{1,0:T(8,128)(2,1)}, u32[]{:S(2)}) copy-start(bf16[128,2048]{1,0:T(8,128)(2,1)} %v_ref.1) | copy-start | bytes 1572868
  3.8 1.0 %copy-start.3 = (bf16[128,2048]{1,0:T(8,128)(2,1)S(1)}, bf16[128,2048]{1,0:T(8,128)(2,1)}, u32[]{:S(2)}) copy-start(bf16[128,2048]{1,0:T(8,128)(2,1)} %g_ref.1) | copy-start | bytes 1572868
  4.8 0.7 %copy-start.4 = (s32[16]{0:T(128)S(1)}, s32[16]{0:T(128)}, u32[]{:S(2)}) copy-start(s32[16]{0:T(128)} %lengths_ref.1) | copy-start | bytes 196

commit v2 on v1

--- a/solution.py
+++ b/solution.py
@@ -131,10 +131,12 @@
 
 
 def bounded_kernel(
-    count, lengths_ref, q_ref, k_ref, v_ref, g_ref,
+    count, lengths_hbm, q_hbm, k_hbm, v_hbm, g_hbm,
     attended_ref, query_grad_ref, key_grad_ref, value_grad_ref,
-    state, near, far, part, pair_mask, first_mask, last_mask,
-    own_send, pass_send, far_send, near_recv, far_recv,
+    lengths_ref, q_ref, k_ref, v_ref, g_ref,
+    state, near, far, aside, part, pair_mask, first_mask, last_mask,
+    load, own_send, pass_send, aside_send, relay_send, aside_recv,
+    far_send, near_recv, far_recv,
 ):
     tokens, width = q_ref.shape
     heads = width // DH
@@ -148,6 +150,22 @@
     takes = jnp.where(parity == 0, behind, ahead)
     passes = jnp.where(parity == 0, ahead, behind)
 
+    row, row_count = lax.div(block, 2), count // 2
+    onward = block + 2 - 4 * parity
+    aside_end = jnp.where(parity == 0, row, row_count - 1 - row) * chunks // row_count
+    relay_end = jnp.where(parity == 0, row_count - 1 - row, row) * chunks // row_count
+    pass_start = jnp.where(parity == 0, row + 1, row_count - row) * chunks // row_count
+
+    loads = [
+        pltpu.make_async_copy(source, target, load.at[n])
+        for n, (source, target) in enumerate([
+            (lengths_hbm, lengths_ref), (k_hbm, k_ref), (v_hbm, v_ref),
+            (q_hbm, q_ref), (g_hbm, g_ref),
+        ])
+    ]
+    for copy in loads:
+        copy.start()
+
     barrier = pltpu.get_barrier_semaphore()
     pl.semaphore_signal(barrier, inc=1, device_id={"seq": partner})
 
@@ -159,6 +177,7 @@
     def _():
         pl.semaphore_signal(barrier, inc=1, device_id={"seq": block + 2})
 
+    loads[0].wait()
     first_pos = block * tokens
     rows = lax.broadcasted_iota(jnp.int32, (tokens, tokens), 0)
     columns = lax.broadcasted_iota(jnp.int32, (tokens, tokens), 1)
@@ -217,6 +236,18 @@
             pass_send.at[i], near_recv.at[1 - parity, i], device_id={"seq": partner},
         )
 
+    def aside_copy(i):
+        return pltpu.make_async_remote_copy(
+            state.at[1 - parity, span(i)], aside.at[span(i)],
+            aside_send.at[i], aside_recv.at[i], device_id={"seq": partner},
+        )
+
+    def relay_copy(i):
+        return pltpu.make_async_remote_copy(
+            aside.at[span(i)], near.at[parity, span(i)],
+            relay_send.at[i], near_recv.at[parity, i], device_id={"seq": onward},
+        )
+
     def far_copy(kind, i):
         return pltpu.make_async_remote_copy(
             state.at[kind, span(i)], far.at[kind, span(i)],
@@ -240,12 +271,17 @@
         def _():
             far_copy(1, i).start()
 
+        @pl.when(i < aside_end)
+        def _():
+            aside_copy(i).start()
+
         own_copy(i).start()
 
+    for copy in loads[1:]:
+        copy.wait()
     states(0)
-    pl.semaphore_wait(
-        barrier, 1 + jnp.where(behind, one, zero) + jnp.where(ahead, one, zero)
-    )
+    neighbours = jnp.where(behind, one, zero) + jnp.where(ahead, one, zero)
+    pl.semaphore_wait(barrier, 1 + neighbours)
     send(0)
 
     @pl.loop(1, chunks)
@@ -279,24 +315,23 @@
             part[2, h] = dot(grads, q, rows_rows)
             part[3, h] = dot(scores, g, rows_rows)
 
-        @pl.when(passes)
-        def _():
-            far_copy(1 - parity, i).wait_recv()
-            pass_copy(i).start()
+        @pl.when(i < relay_end)
+        def _():
+            aside_copy(i).wait_recv()
+            relay_copy(i).start()
+
+        @pl.when(i + pass_start < chunks)
+        def _():
+            far_copy(1 - parity, i + pass_start).wait_recv()
+            pass_copy(i + pass_start).start()
 
     @pl.loop(0, chunks)
     def _(i):
-        own_copy(i).wait_send()
-
-        @pl.when(ahead)
-        def _():
-            far_copy(0, i).wait_send()
-
-        @pl.when(behind)
-        def _():
-            far_copy(1, i).wait_send()
-
         pass_copy(i).wait_recv()
+
+        @pl.when(passes & (i < pass_start))
+        def _():
+            far_copy(1 - parity, i).wait_recv()
 
         @pl.when(takes)
         def _():
@@ -328,11 +363,40 @@
                 part[3, h] + (dot(k, later, plain) + dot(k, later_low, plain))
             ).astype(jnp.bfloat16)
 
-    @pl.when(passes)
-    def _():
-        @pl.loop(0, chunks)
-        def _(i):
+    @pl.loop(0, chunks)
+    def _(i):
+        own_copy(i).wait_send()
+
+        @pl.when(ahead)
+        def _():
+            far_copy(0, i).wait_send()
+
+        @pl.when(behind)
+        def _():
+            far_copy(1, i).wait_send()
+
+        @pl.when(i < aside_end)
+        def _():
+            aside_copy(i).wait_send()
+
+        @pl.when(i < relay_end)
+        def _():
+            relay_copy(i).wait_send()
+
+        @pl.when(i >= pass_start)
+        def _():
             pass_copy(i).wait_send()
+
+
+def store_kernel(*refs):
+    sources, targets, done = refs[:4], refs[4:8], refs[8]
+    copies = [
+        pltpu.make_async_copy(sources[n], targets[n], done.at[n]) for n in range(4)
+    ]
+    for copy in copies:
+        copy.start()
+    for copy in copies:
+        copy.wait()
 
 
 def local_bounded(queries, key_rows, value_rows, out_grad, lengths):
@@ -341,17 +405,27 @@
     chunks = heads // CHUNK_HEADS
     whole = pl.BlockSpec(memory_space=pltpu.VMEM)
     states = pltpu.VMEM((2, heads, DH, DH), jnp.float32)
-    return tuple(pl.pallas_call(
+    apart = pl.BlockSpec(memory_space=pltpu.HBM)
+    rows = pltpu.VMEM((tokens, width), jnp.bfloat16)
+    outs = [jax.ShapeDtypeStruct((tokens, width), jnp.bfloat16)] * 4
+    results = pl.pallas_call(
         functools.partial(bounded_kernel, lax.axis_size("seq")),
-        out_shape=[jax.ShapeDtypeStruct((tokens, width), jnp.bfloat16)] * 4,
-        in_specs=[pl.BlockSpec(memory_space=pltpu.SMEM)] + [whole] * 4,
+        out_shape=[pltpu.VMEM((tokens, width), jnp.bfloat16)] * 4,
+        in_specs=[apart] * 5,
         out_specs=[whole] * 4,
         scratch_shapes=[
+            pltpu.SMEM((DOCS,), jnp.int32),
+            rows, rows, rows, rows,
             states, states, states,
+            pltpu.VMEM((heads, DH, DH), jnp.float32),
             pltpu.VMEM((4, heads, tokens, DH), jnp.float32),
             pltpu.VMEM((tokens, tokens), jnp.float32),
             pltpu.VMEM((tokens, DH), jnp.bfloat16),
             pltpu.VMEM((tokens, DH), jnp.bfloat16),
+            pltpu.SemaphoreType.DMA((5,)),
+            pltpu.SemaphoreType.DMA((chunks,)),
+            pltpu.SemaphoreType.DMA((chunks,)),
+            pltpu.SemaphoreType.DMA((chunks,)),
             pltpu.SemaphoreType.DMA((chunks,)),
             pltpu.SemaphoreType.DMA((chunks,)),
             pltpu.SemaphoreType.DMA((2, chunks)),
@@ -359,9 +433,20 @@
             pltpu.SemaphoreType.DMA((2, chunks)),
         ],
         compiler_params=pltpu.CompilerParams(
-            collective_id=0, has_side_effects=True, vmem_limit_bytes=40 * 2**20
+            collective_id=0, has_side_effects=True, vmem_limit_bytes=60 * 2**20
         ),
-    )(lengths, queries, key_rows, value_rows, out_grad))
+    )(lengths, queries, key_rows, value_rows, out_grad)
+    return tuple(pl.pallas_call(
+        store_kernel,
+        out_shape=outs,
+        in_specs=[pl.BlockSpec(memory_space=pl.ANY)] * 4,
+        out_specs=[apart] * 4,
+        scratch_shapes=[pltpu.SemaphoreType.DMA((4,))],
+        compiler_params=pltpu.CompilerParams(vmem_limit_bytes=2**20),
+        cost_estimate=pl.CostEstimate(
+            flops=0, bytes_accessed=16 * tokens * width, transcendentals=0
+        ),
+    )(*results))
 
 
 def local(queries, key_rows, value_rows, out_grad, lengths):

time: 59 us -> 48.3 us (0.82)
  the two profiles are of different devices: /device:TPU:8 before, /device:TPU:0 now
where the time goes in v2:
time: 48.3 us; the launch traced here: 48.1 us
  Pallas kernels  47.5 us (98%)
  between operations  0.64 us (1%)
    pallas_call x1, Pallas kernels, local_bounded(): pl.pallas_call(functools.partial(bounded_kernel, lax.axis_size('seq')), o...  46.1 us
    pallas_call x1, Pallas kernels, local_bounded(): pl.pallas_call(store_kernel, out_shape=outs, in_specs=[pl.BlockSpec(memor...  1.35 us

profile of v2, /device:TPU:0, one launch (start us, length us, event | category | flops | bytes accessed | tf_op | source)
XLA Modules:
  0.0 48.1 jit_solution(989606868707663728)
XLA Ops:
  0.6 46.1 %shard_map.84 = (bf16[128,2048]{1,0:T(8,128)(2,1)S(1)}, bf16[128,2048]{1,0:T(8,128)(2,1)S(1)}, bf16[128,2048]{1,0:T(8,128)(2,1)S(1)}, bf16[128,2048]{1,0:T(8,128)(2,1)S(1)}) custom-call(s32[16]{0:T(128)} %lengths_hbm.1, bf16[128,2048]{1,0:T(8,128)(2,1)} %q_hbm.1, bf16[128,2048]{1,0:T(8,128)(2,1)} %k_hbm.1, bf16[128,2048]{1,0:T(8,128)(2,1)} %v_hbm.1, ...), custom_call_target="tpu_custom_call" | custom-call | tf_op jit(solution)/shard_map/pallas_call | solution.py:411
  46.8 1.3 %shard_map.85 = (bf16[128,2048]{1,0:T(8,128)(2,1)}, bf16[128,2048]{1,0:T(8,128)(2,1)}, bf16[128,2048]{1,0:T(8,128)(2,1)}, bf16[128,2048]{1,0:T(8,128)(2,1)}) custom-call(bf16[128,2048]{1,0:T(8,128)(2,1)S(1)} %get-tuple-element.8.refs_0_, bf16[128,2048]{1,0:T(8,128)(2,1)S(1)} %get-tuple-element.9.refs_1_, bf16[128,2048]{1,0:T(8,128)(2,1)S(1)} %get-tuple-element.10.refs_2_, ...), custom_call_target="tpu_custom_call" | custom-call | bytes 4194304 | tf_op jit(solution)/shard_map/pallas_call | solution.py:439

commit v3 on v2

--- a/solution.py
+++ b/solution.py
@@ -127,7 +127,7 @@
     )
 
 
-CHUNK_HEADS = 2
+CHUNK_HEADS = 4
 
 
 def bounded_kernel(
@@ -135,7 +135,7 @@
     attended_ref, query_grad_ref, key_grad_ref, value_grad_ref,
     lengths_ref, q_ref, k_ref, v_ref, g_ref,
     state, near, far, aside, part, pair_mask, first_mask, last_mask,
-    load, own_send, pass_send, aside_send, relay_send, aside_recv,
+    load, own_send, cross_send, aside_send, relay_send, aside_recv,
     far_send, near_recv, far_recv,
 ):
     tokens, width = q_ref.shape
@@ -152,55 +152,56 @@
 
     row, row_count = lax.div(block, 2), count // 2
     onward = block + 2 - 4 * parity
+    across = block - 1 + 2 * parity
     aside_end = jnp.where(parity == 0, row, row_count - 1 - row) * chunks // row_count
     relay_end = jnp.where(parity == 0, row_count - 1 - row, row) * chunks // row_count
-    pass_start = jnp.where(parity == 0, row + 1, row_count - row) * chunks // row_count
-
-    loads = [
-        pltpu.make_async_copy(source, target, load.at[n])
-        for n, (source, target) in enumerate([
-            (lengths_hbm, lengths_ref), (k_hbm, k_ref), (v_hbm, v_ref),
-            (q_hbm, q_ref), (g_hbm, g_ref),
-        ])
+
+    barrier = pltpu.get_barrier_semaphore()
+    pl.semaphore_signal(barrier, inc=1, device_id={"seq": partner})
+
+    @pl.when(behind)
+    def _():
+        pl.semaphore_signal(barrier, inc=1, device_id={"seq": block - 2})
+
+    @pl.when(ahead)
+    def _():
+        pl.semaphore_signal(barrier, inc=1, device_id={"seq": block + 2})
+
+    @pl.when(takes)
+    def _():
+        pl.semaphore_signal(barrier, inc=1, device_id={"seq": across})
+
+    early = pl.ds(0, CHUNK_HEADS * DH)
+    late = pl.ds(CHUNK_HEADS * DH, width - CHUNK_HEADS * DH)
+    pairs = [(k_hbm, k_ref), (v_hbm, v_ref), (q_hbm, q_ref), (g_hbm, g_ref)]
+    loads = [pltpu.make_async_copy(lengths_hbm, lengths_ref, load.at[0])] + [
+        pltpu.make_async_copy(source.at[:, at], target.at[:, at], load.at[1 + n + m])
+        for n, at in ((0, early), (4, late))
+        for m, (source, target) in enumerate(pairs)
     ]
     for copy in loads:
         copy.start()
 
-    barrier = pltpu.get_barrier_semaphore()
-    pl.semaphore_signal(barrier, inc=1, device_id={"seq": partner})
-
-    @pl.when(behind)
-    def _():
-        pl.semaphore_signal(barrier, inc=1, device_id={"seq": block - 2})
-
-    @pl.when(ahead)
-    def _():
-        pl.semaphore_signal(barrier, inc=1, device_id={"seq": block + 2})
-
     loads[0].wait()
     first_pos = block * tokens
     rows = lax.broadcasted_iota(jnp.int32, (tokens, tokens), 0)
-    columns = lax.broadcasted_iota(jnp.int32, (tokens, tokens), 1)
-    row_doc = jnp.zeros((tokens, tokens), jnp.int32)
-    column_doc = jnp.zeros((tokens, tokens), jnp.int32)
     zero, one = jnp.int32(0), jnp.int32(1)
-    first_doc = last_doc = opens_first = opens_next = zero
-    opens_before = opens_after = zero
-    end = zero
+    opens_first = opens_next = opens_before = opens_after = zero
+    first_stop, last_start = jnp.int32(tokens), zero
+    stops = []
+    stop = -first_pos
     for doc in range(DOCS):
-        start = end - first_pos
-        end = end + lengths_ref[doc]
-        stop = end - first_pos
-        row_doc += jnp.where(stop <= rows, 1, 0)
-        column_doc += jnp.where(stop <= columns, 1, 0)
-        first_doc += jnp.where(stop <= 0, one, zero)
-        last_doc += jnp.where(stop <= tokens - 1, one, zero)
-        opens_first = jnp.maximum(opens_first, jnp.where(start == 0, one, zero))
-        opens_next = jnp.maximum(opens_next, jnp.where(start == tokens, one, zero))
-        before = (start >= -tokens) & (start < 0)
-        after = (start >= tokens) & (start < 2 * tokens)
-        opens_before = jnp.maximum(opens_before, jnp.where(before, one, zero))
-        opens_after = jnp.maximum(opens_after, jnp.where(after, one, zero))
+        start = stop
+        stop = start + lengths_ref[doc]
+        stops.append(stop)
+        first_stop = jnp.where(stop > 0, jnp.minimum(first_stop, stop), first_stop)
+        last_start = jnp.where(start < tokens, jnp.maximum(last_start, start), last_start)
+        opens_first = jnp.where(start == 0, one, opens_first)
+        opens_next = jnp.where(start == tokens, one, opens_next)
+        opens_before = jnp.where((start >= -tokens) & (start < 0), one, opens_before)
+        opens_after = jnp.where(
+            (start >= tokens) & (start < 2 * tokens), one, opens_after
+        )
     near_weight = [
         factor * (1 - opens_first).astype(jnp.float32),
         factor * (1 - opens_next).astype(jnp.float32),
@@ -209,9 +210,8 @@
         near_weight[0] * (1 - opens_before).astype(jnp.float32),
         near_weight[1] * (1 - opens_after).astype(jnp.float32),
     ]
-    pair_mask[...] = jnp.where((columns <= rows) & (row_doc == column_doc), factor, 0.0)
-    first_mask[...] = jnp.where(row_doc == first_doc, 1.0, 0.0).astype(jnp.bfloat16)
-    last_mask[...] = jnp.where(row_doc == last_doc, 1.0, 0.0).astype(jnp.bfloat16)
+    first_mask[...] = jnp.where(rows < first_stop, 1.0, 0.0).astype(jnp.bfloat16)
+    last_mask[...] = jnp.where(rows >= last_start, 1.0, 0.0).astype(jnp.bfloat16)
 
     def span(i):
         return pl.ds(i * CHUNK_HEADS, CHUNK_HEADS)
@@ -230,10 +230,10 @@
             own_send.at[i], near_recv.at[parity, i], device_id={"seq": partner},
         )
 
-    def pass_copy(i):
+    def cross_copy(i):
         return pltpu.make_async_remote_copy(
-            far.at[1 - parity, span(i)], near.at[1 - parity, span(i)],
-            pass_send.at[i], near_recv.at[1 - parity, i], device_id={"seq": partner},
+            state.at[1 - parity, span(i)], near.at[1 - parity, span(i)],
+            cross_send.at[i], near_recv.at[1 - parity, i], device_id={"seq": across},
         )
 
     def aside_copy(i):
@@ -275,19 +275,33 @@
         def _():
             aside_copy(i).start()
 
+        @pl.when(takes & (i >= aside_end))
+        def _():
+            cross_copy(i).start()
+
         own_copy(i).start()
 
-    for copy in loads[1:]:
+    for copy in loads[1:5]:
         copy.wait()
     states(0)
     neighbours = jnp.where(behind, one, zero) + jnp.where(ahead, one, zero)
-    pl.semaphore_wait(barrier, 1 + neighbours)
+    pl.semaphore_wait(barrier, 1 + neighbours + jnp.where(takes, one, zero))
     send(0)
+    for copy in loads[5:]:
+        copy.wait()
 
     @pl.loop(1, chunks)
     def _(i):
         states(i)
         send(i)
+
+    columns = lax.broadcasted_iota(jnp.int32, (tokens, tokens), 1)
+    row_doc = jnp.zeros((tokens, tokens), jnp.int32)
+    column_doc = jnp.zeros((tokens, tokens), jnp.int32)
+    for stop in stops:
+        row_doc += jnp.where(stop <= rows, 1, 0)
+        column_doc += jnp.where(stop <= columns, 1, 0)
+    pair_mask[...] = jnp.where((columns <= rows) & (row_doc == column_doc), factor, 0.0)
 
     @pl.when(jnp.logical_not(takes))
     def _():
@@ -320,16 +334,11 @@
             aside_copy(i).wait_recv()
             relay_copy(i).start()
 
-        @pl.when(i + pass_start < chunks)
-        def _():
-            far_copy(1 - parity, i + pass_start).wait_recv()
-            pass_copy(i + pass_start).start()
-
     @pl.loop(0, chunks)
     def _(i):
-        pass_copy(i).wait_recv()
-
-        @pl.when(passes & (i < pass_start))
+        cross_copy(i).wait_recv()
+
+        @pl.when(passes)
         def _():
             far_copy(1 - parity, i).wait_recv()
 
@@ -383,9 +392,9 @@
         def _():
             relay_copy(i).wait_send()
 
-        @pl.when(i >= pass_start)
-        def _():
-            pass_copy(i).wait_send()
+        @pl.when(takes & (i >= aside_end))
+        def _():
+            cross_copy(i).wait_send()
 
 
 def store_kernel(*refs):
@@ -422,7 +431,7 @@
             pltpu.VMEM((tokens, tokens), jnp.float32),
             pltpu.VMEM((tokens, DH), jnp.bfloat16),
             pltpu.VMEM((tokens, DH), jnp.bfloat16),
-            pltpu.SemaphoreType.DMA((5,)),
+            pltpu.SemaphoreType.DMA((9,)),
             pltpu.SemaphoreType.DMA((chunks,)),
             pltpu.SemaphoreType.DMA((chunks,)),
             pltpu.SemaphoreType.DMA((chunks,)),

time: 48.3 us -> 47.8 us (0.990)
  Pallas kernels: 47.5 us -> 47 us
    pallas_call x1, Pallas kernels: 46.1 us -> 45.6 us  [local_bounded(): pl.pallas_call(functools.partial(bounded_kernel, lax.axis_size('seq')), o...]
where the time goes in v3:
time: 47.8 us; the launch traced here: 47.6 us
  Pallas kernels  47 us (98%)
  between operations  0.64 us (1%)
    pallas_call x1, Pallas kernels, local_bounded(): pl.pallas_call(functools.partial(bounded_kernel, lax.axis_size('seq')), o...  45.6 us
    pallas_call x1, Pallas kernels, local_bounded(): pl.pallas_call(store_kernel, out_shape=outs, in_specs=[pl.BlockSpec(memor...  1.35 us

profile of v3, /device:TPU:0, one launch (start us, length us, event | category | flops | bytes accessed | tf_op | source)
XLA Modules:
  0.0 47.6 jit_solution(1054788492431255619)
XLA Ops:
  0.6 45.6 %shard_map.84 = (bf16[128,2048]{1,0:T(8,128)(2,1)S(1)}, bf16[128,2048]{1,0:T(8,128)(2,1)S(1)}, bf16[128,2048]{1,0:T(8,128)(2,1)S(1)}, bf16[128,2048]{1,0:T(8,128)(2,1)S(1)}) custom-call(s32[16]{0:T(128)} %lengths_hbm.1, bf16[128,2048]{1,0:T(8,128)(2,1)} %q_hbm.1, bf16[128,2048]{1,0:T(8,128)(2,1)} %k_hbm.1, bf16[128,2048]{1,0:T(8,128)(2,1)} %v_hbm.1, ...), custom_call_target="tpu_custom_call" | custom-call | tf_op jit(solution)/shard_map/pallas_call | solution.py:420
  46.3 1.3 %shard_map.85 = (bf16[128,2048]{1,0:T(8,128)(2,1)}, bf16[128,2048]{1,0:T(8,128)(2,1)}, bf16[128,2048]{1,0:T(8,128)(2,1)}, bf16[128,2048]{1,0:T(8,128)(2,1)}) custom-call(bf16[128,2048]{1,0:T(8,128)(2,1)S(1)} %get-tuple-element.8.refs_0_, bf16[128,2048]{1,0:T(8,128)(2,1)S(1)} %get-tuple-element.9.refs_1_, bf16[128,2048]{1,0:T(8,128)(2,1)S(1)} %get-tuple-element.10.refs_2_, ...), custom_call_target="tpu_custom_call" | custom-call | bytes 4194304 | tf_op jit(solution)/shard_map/pallas_call | solution.py:448

commit v4 on v3

--- a/solution.py
+++ b/solution.py
@@ -127,7 +127,8 @@
     )
 
 
-CHUNK_HEADS = 4
+SIZES = (1, 3, 4, 4, 2, 2)
+STARTS = (0, 1, 4, 8, 12, 14)
 
 
 def bounded_kernel(
@@ -140,7 +141,7 @@
 ):
     tokens, width = q_ref.shape
     heads = width // DH
-    chunks = heads // CHUNK_HEADS
+    chunks = len(SIZES)
     factor = (DH * tokens * count / DOCS) ** -0.5
     block = lax.axis_index("seq")
     parity = lax.rem(block, 2)
@@ -153,8 +154,8 @@
     row, row_count = lax.div(block, 2), count // 2
     onward = block + 2 - 4 * parity
     across = block - 1 + 2 * parity
-    aside_end = jnp.where(parity == 0, row, row_count - 1 - row) * chunks // row_count
-    relay_end = jnp.where(parity == 0, row_count - 1 - row, row) * chunks // row_count
+    aside_end = jnp.where(parity == 0, row, row_count - 1 - row) * heads // row_count
+    relay_end = jnp.where(parity == 0, row_count - 1 - row, row) * heads // row_count
 
     barrier = pltpu.get_barrier_semaphore()
     pl.semaphore_signal(barrier, inc=1, device_id={"seq": partner})
@@ -171,8 +172,8 @@
     def _():
         pl.semaphore_signal(barrier, inc=1, device_id={"seq": across})
 
-    early = pl.ds(0, CHUNK_HEADS * DH)
-    late = pl.ds(CHUNK_HEADS * DH, width - CHUNK_HEADS * DH)
+    early = pl.ds(0, SIZES[0] * DH)
+    late = pl.ds(SIZES[0] * DH, width - SIZES[0] * DH)
     pairs = [(k_hbm, k_ref), (v_hbm, v_ref), (q_hbm, q_ref), (g_hbm, g_ref)]
     loads = [pltpu.make_async_copy(lengths_hbm, lengths_ref, load.at[0])] + [
         pltpu.make_async_copy(source.at[:, at], target.at[:, at], load.at[1 + n + m])
@@ -214,10 +215,10 @@
     last_mask[...] = jnp.where(rows >= last_start, 1.0, 0.0).astype(jnp.bfloat16)
 
     def span(i):
-        return pl.ds(i * CHUNK_HEADS, CHUNK_HEADS)
+        return pl.ds(STARTS[i], SIZES[i])
 
     def lanes(h):
-        return pl.ds(pl.multiple_of(h * DH, DH), DH)
+        return pl.ds(h * DH, DH)
 
     def dot(a, b, dims):
         return lax.dot_general(a, b, (dims, ((), ())), preferred_element_type=jnp.float32)
@@ -256,8 +257,7 @@
         )
 
     def states(i):
-        for j in range(CHUNK_HEADS):
-            h = i * CHUNK_HEADS + j
+        for h in range(STARTS[i], STARTS[i] + SIZES[i]):
             at = lanes(h)
             state[0, h] = dot(k_ref[:, at] * last_mask[...], v_ref[:, at], rows_rows)
             state[1, h] = dot(q_ref[:, at] * first_mask[...], g_ref[:, at], rows_rows)
@@ -271,11 +271,11 @@
         def _():
             far_copy(1, i).start()
 
-        @pl.when(i < aside_end)
+        @pl.when(STARTS[i] < aside_end)
         def _():
             aside_copy(i).start()
 
-        @pl.when(takes & (i >= aside_end))
+        @pl.when(takes & (STARTS[i] >= aside_end))
         def _():
             cross_copy(i).start()
 
@@ -290,8 +290,7 @@
     for copy in loads[5:]:
         copy.wait()
 
-    @pl.loop(1, chunks)
-    def _(i):
+    for i in range(1, chunks):
         states(i)
         send(i)
 
@@ -316,10 +315,8 @@
         def _(h):
             far[1 - parity, h] = jnp.zeros((DH, DH), jnp.float32)
 
-    @pl.loop(0, chunks)
-    def _(i):
-        for j in range(CHUNK_HEADS):
-            h = i * CHUNK_HEADS + j
+    for i in range(chunks):
+        for h in range(STARTS[i], STARTS[i] + SIZES[i]):
             at = lanes(h)
             q, k, v, g = q_ref[:, at], k_ref[:, at], v_ref[:, at], g_ref[:, at]
             scores = (dot(q, k, turned) * pair_mask[...]).astype(jnp.bfloat16)
@@ -329,13 +326,12 @@
             part[2, h] = dot(grads, q, rows_rows)
             part[3, h] = dot(scores, g, rows_rows)
 
-        @pl.when(i < relay_end)
+        @pl.when(STARTS[i] < relay_end)
         def _():
             aside_copy(i).wait_recv()
             relay_copy(i).start()
 
-    @pl.loop(0, chunks)
-    def _(i):
+    for i in range(chunks):
         cross_copy(i).wait_recv()
 
         @pl.when(passes)
@@ -347,8 +343,7 @@
             far_copy(parity, i).wait_recv()
             own_copy(i).wait_recv()
 
-        for j in range(CHUNK_HEADS):
-            h = i * CHUNK_HEADS + j
+        for h in range(STARTS[i], STARTS[i] + SIZES[i]):
             at = lanes(h)
             mixed = []
             for kind in range(2):
@@ -372,8 +367,7 @@
                 part[3, h] + (dot(k, later, plain) + dot(k, later_low, plain))
             ).astype(jnp.bfloat16)
 
-    @pl.loop(0, chunks)
-    def _(i):
+    for i in range(chunks):
         own_copy(i).wait_send()
 
         @pl.when(ahead)
@@ -384,15 +378,15 @@
         def _():
             far_copy(1, i).wait_send()
 
-        @pl.when(i < aside_end)
+        @pl.when(STARTS[i] < aside_end)
         def _():
             aside_copy(i).wait_send()
 
-        @pl.when(i < relay_end)
+        @pl.when(STARTS[i] < relay_end)
         def _():
             relay_copy(i).wait_send()
 
-        @pl.when(takes & (i >= aside_end))
+        @pl.when(takes & (STARTS[i] >= aside_end))
         def _():
             cross_copy(i).wait_send()
 
@@ -411,7 +405,7 @@
 def local_bounded(queries, key_rows, value_rows, out_grad, lengths):
     tokens, width = queries.shape
     heads = width // DH
-    chunks = heads // CHUNK_HEADS
+    chunks = len(SIZES)
     whole = pl.BlockSpec(memory_space=pltpu.VMEM)
     states = pltpu.VMEM((2, heads, DH, DH), jnp.float32)
     apart = pl.BlockSpec(memory_space=pltpu.HBM)
@@ -460,7 +454,7 @@
 
 def local(queries, key_rows, value_rows, out_grad, lengths):
     count = lax.axis_size("seq")
-    if count == 8 and queries.shape[0] == DH:
+    if count == 8 and queries.shape == (DH, 16 * DH):
         return local_bounded(queries, key_rows, value_rows, out_grad, lengths)
     return local_general(queries, key_rows, value_rows, out_grad, lengths)
 

time: 47.8 us -> 47.6 us (level)
  no operation moved by 1% of the time
where the time goes in v4:
time: 47.6 us; the launch traced here: 47.4 us
  Pallas kernels  46.8 us (98%)
  between operations  0.64 us (1%)
    pallas_call x1, Pallas kernels, local_bounded(): pl.pallas_call(functools.partial(bounded_kernel, lax.axis_size('seq')), o...  45.4 us
    pallas_call x1, Pallas kernels, local_bounded(): pl.pallas_call(store_kernel, out_shape=outs, in_specs=[pl.BlockSpec(memor...  1.35 us

profile of v4, /device:TPU:0, one launch (start us, length us, event | category | flops | bytes accessed | tf_op | source)
XLA Modules:
  0.0 47.4 jit_solution(18371202234413633133)
XLA Ops:
  0.6 45.4 %shard_map.84 = (bf16[128,2048]{1,0:T(8,128)(2,1)S(1)}, bf16[128,2048]{1,0:T(8,128)(2,1)S(1)}, bf16[128,2048]{1,0:T(8,128)(2,1)S(1)}, bf16[128,2048]{1,0:T(8,128)(2,1)S(1)}) custom-call(s32[16]{0:T(128)} %lengths_hbm.1, bf16[128,2048]{1,0:T(8,128)(2,1)} %q_hbm.1, bf16[128,2048]{1,0:T(8,128)(2,1)} %k_hbm.1, bf16[128,2048]{1,0:T(8,128)(2,1)} %v_hbm.1, ...), custom_call_target="tpu_custom_call" | custom-call | tf_op jit(solution)/shard_map/pallas_call | solution.py:414
  46.0 1.3 %shard_map.85 = (bf16[128,2048]{1,0:T(8,128)(2,1)}, bf16[128,2048]{1,0:T(8,128)(2,1)}, bf16[128,2048]{1,0:T(8,128)(2,1)}, bf16[128,2048]{1,0:T(8,128)(2,1)}) custom-call(bf16[128,2048]{1,0:T(8,128)(2,1)S(1)} %get-tuple-element.8.refs_0_, bf16[128,2048]{1,0:T(8,128)(2,1)S(1)} %get-tuple-element.9.refs_1_, bf16[128,2048]{1,0:T(8,128)(2,1)S(1)} %get-tuple-element.10.refs_2_, ...), custom_call_target="tpu_custom_call" | custom-call | bytes 4194304 | tf_op jit(solution)/shard_map/pallas_call | solution.py:442
